TPU v7x, 32 devices: a whole 2x2x4 slice. The times are simulated.
32 devices in a mesh: grp: 2 (over y), seq: 4 (over z), head: 2 (over x), sub: 2 (over core).
Axes of the slice: x: 2, y: 2, z: 4, core: 2. Of those that a mesh axis runs over, the one named last changes fastest.
Arguments:
- queries: bfloat16 [4096, 64, 128], P(('grp', 'seq'), ('head', 'sub')), parts along dimension 0, may hold values from -6 to 6
- key_rows: bfloat16 [4096, 64, 128], P(('grp', 'seq'), ('head', 'sub')), parts along dimension 0, may hold values from -6 to 6
- value_rows: bfloat16 [4096, 64, 128], P(('grp', 'seq'), ('head', 'sub')), parts along dimension 0, may hold values from -6 to 6
- out_adjoint: bfloat16 [4096, 64, 128], P(('grp', 'seq'), ('head', 'sub')), parts along dimension 0, may hold values from -6 to 6
Outputs:
- attended: bfloat16 [4096, 64, 128], P(('grp', 'seq'), ('head', 'sub')), parts along dimension 0
- query_grad: bfloat16 [4096, 64, 128], P(('grp', 'seq', 'head', 'sub')), parts along dimension 0
- key_grad: bfloat16 [4096, 64, 128], P(('grp', 'seq', 'head', 'sub')), parts along dimension 0
- value_grad: bfloat16 [4096, 64, 128], P(('grp', 'seq', 'head', 'sub')), parts along dimension 0
There are 2 independent parts, one for each index of `grp`. A program takes and returns all parts, laid end to end along the dimension named above; each array names one. Nothing has to cross between parts.
All inputs are finite; a program needn't handle non-finite values.
Results may differ from a plain program's by a relative error of at most 0.0058.
Values may be sent and summed in bfloat16 or wider, within the bound.
A program may use at most 128 MiB of HBM per device.

v0:
```python
import jax
import jax.numpy as jnp
from jax import lax
from jax.sharding import PartitionSpec as P

SPAN = 64


def prefix(part, axis, combine, identity, reverse):
    count = lax.axis_size(axis)
    place = lax.axis_index(axis)
    ahead = count - 1 - place if reverse else place
    gathered = lax.all_gather(part, axis)
    state = jnp.zeros_like(part) + jnp.asarray(identity, part.dtype)

    def one(turn, state):
        source = count - 1 - turn if reverse else turn
        return combine(state, lax.dynamic_index_in_dim(gathered, source, 0, False))

    return lax.fori_loop(0, ahead, one, state)


def add_states(earlier, later):
    return earlier + later


def per_device(queries, key_rows, value_rows, out_adjoint):
    tok_dev, heads_dev, head_dim = queries.shape
    span = SPAN
    blocks = tok_dev // span
    offset = lax.axis_index("seq") * tok_dev
    position = offset + jnp.arange(tok_dev, dtype=jnp.int32)
    factor = lax.rsqrt(jnp.float32(head_dim) * (position + 1).astype(jnp.float32))
    scaled = (queries.astype(jnp.float32) * factor[:, None, None]).astype(jnp.bfloat16)
    qsc = scaled.reshape(blocks, span, heads_dev, head_dim)
    kch = key_rows.reshape(blocks, span, heads_dev, head_dim)
    vch = value_rows.reshape(blocks, span, heads_dev, head_dim)
    dch = out_adjoint.reshape(blocks, span, heads_dev, head_dim)
    kv_block = jnp.einsum("nchd,nche->nhde", kch, vch, preferred_element_type=jnp.float32)
    adj_block = jnp.einsum("nche,nchd->nhed", dch, qsc, preferred_element_type=jnp.float32)
    kv_total = jnp.sum(kv_block, 0)
    adj_total = jnp.sum(adj_block, 0)
    zeros = jnp.zeros_like(kv_total)
    before = prefix(kv_total, "seq", add_states, zeros, False)
    after = prefix(adj_total, "seq", add_states, zeros, True)
    state = before[None] + jnp.cumsum(kv_block, 0) - kv_block
    suffix = after[None] + jnp.cumsum(adj_block[::-1], 0)[::-1] - adj_block
    state_low = state.astype(jnp.bfloat16)
    suffix_low = suffix.astype(jnp.bfloat16)
    row = jnp.arange(span, dtype=jnp.int32)
    causal = (row[:, None] >= row[None, :])[None, None]
    scores = jnp.where(
        causal, jnp.einsum("nchd,nshd->nhcs", qsc, kch, preferred_element_type=jnp.float32), 0.0
    ).astype(jnp.bfloat16)
    attended = jnp.einsum(
        "nchd,nhde->nche", qsc, state_low, preferred_element_type=jnp.float32
    ) + jnp.einsum("nhcs,nshe->nche", scores, vch, preferred_element_type=jnp.float32)
    adj_scores = jnp.where(
        causal, jnp.einsum("nche,nshe->nhcs", dch, vch, preferred_element_type=jnp.float32), 0.0
    ).astype(jnp.bfloat16)
    query_grad = (
        jnp.einsum("nche,nhde->nchd", dch, state_low, preferred_element_type=jnp.float32)
        + jnp.einsum("nhcs,nshd->nchd", adj_scores, kch, preferred_element_type=jnp.float32)
    ) * factor.reshape(blocks, span, 1, 1)
    key_grad = jnp.einsum(
        "nshe,nhed->nshd", vch, suffix_low, preferred_element_type=jnp.float32
    ) + jnp.einsum("nhcs,nchd->nshd", adj_scores, qsc, preferred_element_type=jnp.float32)
    value_grad = jnp.einsum(
        "nshd,nhed->nshe", kch, suffix_low, preferred_element_type=jnp.float32
    ) + jnp.einsum("nhcs,nche->nshe", scores, dch, preferred_element_type=jnp.float32)
    shape = (tok_dev, heads_dev, head_dim)
    attended = attended.reshape(shape).astype(jnp.bfloat16)
    query_grad = query_grad.reshape(shape).astype(jnp.bfloat16)
    key_grad = key_grad.reshape(shape).astype(jnp.bfloat16)
    value_grad = value_grad.reshape(shape).astype(jnp.bfloat16)
    query_out, key_out, value_out = (
        lax.all_to_all(query_grad, ("head", "sub"), split_axis=0, concat_axis=1, tiled=True),
        lax.all_to_all(key_grad, ("head", "sub"), split_axis=0, concat_axis=1, tiled=True),
        lax.all_to_all(value_grad, ("head", "sub"), split_axis=0, concat_axis=1, tiled=True),
    )
    return (attended, query_out, key_out, value_out)


def solution(mesh):
    in_specs = (
        P(("grp", "seq"), ("head", "sub"), None),
        P(("grp", "seq"), ("head", "sub"), None),
        P(("grp", "seq"), ("head", "sub"), None),
        P(("grp", "seq"), ("head", "sub"), None),
    )
    out_specs = (
        P(("grp", "seq"), ("head", "sub"), None),
        P(("grp", "seq", "head", "sub"), None, None),
        P(("grp", "seq", "head", "sub"), None, None),
        P(("grp", "seq", "head", "sub"), None, None),
    )
    return jax.shard_map(
        per_device, mesh=mesh, in_specs=in_specs, out_specs=out_specs, check_vma=False
    )
```

profile of v0, /device:TPU:17, one launch (start us, length us, event | category | flops | bytes accessed | tf_op | source)
XLA Modules:
  0.0 251.7 jit_solution(12167041707173029540)
XLA Ops:
  7.3 2.9 %multiply_convert_fusion = bf16[512,16,128]{2,1,0:T(8,128)(2,1)S(1)} fusion(bf16[512,16,128]{2,1,0:T(8,128)(2,1)} %param.8, f32[512]{0:T(512)S(1)} %multiply_rsqrt_fusion.1), kind=kLoop, calls=%fused_computation.14 | loop fusion | flops 3145728 | bytes 4196352 | tf_op jit(solution)/shard_map/convert_element_type | solution.py:34
  10.2 5.0 %fusion.27 = (f32[16,128,128]{1,2,0:T(8,128)S(1)}, f32[8,16,128,128]{2,3,1,0:T(8,128)}) fusion(bf16[8,64,16,128]{3,2,1,0:T(8,128)(2,1)S(1)} %bitcast.73, bf16[8,64,16,128]{3,2,1,0:T(8,128)(2,1)S(1)} %bitcast.68), kind=kOutput, calls=%fused_computation.42 | convolution fusion | flops 270270464 | bytes 13631488 | tf_op jit(solution)/shard_map/nche,nchd->nhed/dot_general | solution.py:40
  16.5 7.6 %fusion.26 = (f32[16,128,128]{2,1,0:T(8,128)}, f32[8,16,128,128]{3,2,1,0:T(8,128)}) fusion(bf16[8,64,16,128]{3,2,1,0:T(8,128)(2,1)S(1)} %bitcast.64, bf16[8,64,16,128]{3,2,1,0:T(8,128)(2,1)} %bitcast.76), kind=kOutput, calls=%fused_computation.41 | convolution fusion | flops 270270464 | bytes 13631488 | tf_op jit(solution)/shard_map/nchd,nche->nhde/dot_general | solution.py:39
  24.1 8.4 %rev.6 = f32[8,16,128,128]{2,3,1,0:T(8,128)} reverse(f32[8,16,128,128]{2,3,1,0:T(8,128)} %get-tuple-element.104), dimensions={0} | reverse | bytes 16777216 | tf_op jit(solution)/shard_map/rev | solution.py:47
  32.6 4.3 %select_convert_fusion = bf16[8,16,64,64]{3,2,1,0:T(8,128)(2,1)} fusion(pred[64,64]{1,0:T(8,128)(4,1)S(1)} %iota_compare_fusion, bf16[8,64,16,128]{3,2,1,0:T(8,128)(2,1)} %bitcast.72, bf16[8,64,16,128]{3,2,1,0:T(8,128)(2,1)S(1)} %bitcast.66), kind=kOutput, calls=%fused_computation.12 | convolution fusion | flops 135266304 | bytes 5246976 | tf_op jit(solution)/shard_map/nche,nshe->nhcs/dot_general | solution.py:59
  39.4 2.8 %fusion.5 = f32[8,16,64,128]{3,2,1,0:T(8,128)} fusion(bf16[8,16,64,64]{3,2,1,0:T(8,128)(2,1)S(1)} %select_convert_fusion.1, bf16[8,64,16,128]{3,2,1,0:T(8,128)(2,1)S(1)} %bitcast.74), kind=kOutput, calls=%fused_computation.17 | convolution fusion | flops 134217728 | bytes 7340032 | tf_op jit(solution)/shard_map/nhcs,nche->nshe/dot_general | solution.py:70
  42.2 8.3 %fusion.28 = f32[8,16,128,128]{2,3,1,0:T(8,128)} fusion(f32[8,16,128,128]{2,3,1,0:T(8,128)} %rev.6), kind=kOutput, calls=%fused_computation.43 | output fusion | flops 14680064 | bytes 16777216 | tf_op jit(solution)/shard_map/jit(cumsum)/reduce_window_sum | solution.py:47
  50.6 46.4 %all-gather.7.cloned.1.call-done = f32[64,128,128]{2,1,0:T(8,128)} async-done(((f32[16,128,128]{2,1,0:T(8,128)}), f32[64,128,128]{2,1,0:T(8,128)}) %all-gather.7.cloned.1.call-update) | async-done | bytes 4194320 | tf_op jit(solution)/shard_map/all_gather | solution.py:13
  100.1 10.3 %subtract_convert_fusion = bf16[8,16,128,128]{2,3,1,0:T(8,128)(2,1)} fusion(f32[8,16,128,128]{2,3,1,0:T(8,128)} %get-tuple-element.104, f32[8,16,128,128]{2,3,1,0:T(8,128)} %fusion.28, f32[16,128,128]{1,2,0:T(8,128)} %copy.98), kind=kLoop, calls=%fused_computation.2 | loop fusion | flops 6291456 | bytes 22020096 | tf_op jit(solution)/shard_map/convert_element_type | solution.py:49
  110.5 5.3 %fusion.15 = f32[8,16,128,64]{2,3,1,0:T(8,128)S(1)} fusion(bf16[8,16,128,128]{2,3,1,0:T(8,128)(2,1)} %subtract_convert_fusion, bf16[8,64,16,128]{3,2,1,0:T(8,128)(2,1)S(1)} %bitcast.65), kind=kOutput, calls=%fused_computation.27 | convolution fusion | flops 268435456 | bytes 10485760 | tf_op jit(solution)/shard_map/nshe,nhed->nshd/dot_general | solution.py:65
  119.8 5.2 %all-to-all-start.1 = ((bf16[512,16,128]{2,1,0:T(8,128)(2,1)}), bf16[512,16,128]{2,1,0:T(8,128)(2,1)}, u32[]{:S(2)}, u32[]{:S(2)}) async-start(bf16[512,16,128]{2,1,0:T(8,128)(2,1)} %bitcast.81), calls=%async_computation.1 | async-start | bytes 4194304 | tf_op jit(solution)/shard_map/all_to_all | solution.py:78
  125.0 5.3 %fusion = bf16[8,64,16,128]{3,1,2,0:T(8,128)(2,1)S(1)} fusion(f32[8,16,64,128]{3,2,1,0:T(8,128)} %fusion.5, bf16[8,16,128,128]{2,3,1,0:T(8,128)(2,1)} %subtract_convert_fusion, bf16[8,64,16,128]{3,2,1,0:T(8,128)(2,1)} %bitcast.77), kind=kOutput, calls=%fused_computation.5 | convolution fusion | flops 270532608 | bytes 12582912 | tf_op jit(solution)/shard_map/nshd,nhed->nshe/dot_general | solution.py:68
  130.3 2.8 %copy.109 = bf16[8,64,16,128]{3,2,1,0:T(8,128)(2,1)} copy(bf16[8,64,16,128]{3,1,2,0:T(8,128)(2,1)S(1)} %fusion) | data formatting | bytes 4194304 | tf_op jit(solution)/shard_map/convert_element_type | solution.py:75
  133.1 44.8 %all-gather.5.cloned.1.call-done = f32[64,128,128]{2,1,0:T(8,128)} async-done(((f32[16,128,128]{2,1,0:T(8,128)}), f32[64,128,128]{2,1,0:T(8,128)}) %all-gather.5.cloned.1.call-update) | async-done | bytes 4194320 | tf_op jit(solution)/shard_map/all_gather | solution.py:13
  178.0 3.0 %while.22 = (s32[]{:T(128)}, f32[16,128,128]{2,1,0:T(8,128)S(1)}, s32[]{:T(128)}, f32[4,16,128,128]{3,2,1,0:T(8,128)}, s32[]{:T(128)}, /*index=5*/s32[]{:T(128)}, s32[]{:T(128)}) while((s32[]{:T(128)}, f32[16,128,128]{2,1,0:T(8,128)S(1)}, s32[]{:T(128)}, f32[4,16,128,128]{3,2,1,0:T(8,128)}, s32[]{:T(128)}, /*index=5*/s32[]{:T(128)}, ...), condition=%wide.region_2.3_spmd, body=%wide.region_1.0_spmd.sunk | while | flops 262149 | bytes 3145843 | solution.py:20
  181.0 5.1 %all-to-all-start.2 = ((bf16[512,16,128]{2,1,0:T(8,128)(2,1)}), bf16[512,16,128]{2,1,0:T(8,128)(2,1)}, u32[]{:S(2)}, u32[]{:S(2)}) async-start(bf16[512,16,128]{2,1,0:T(8,128)(2,1)} %bitcast.80), calls=%async_computation.2 | async-start | bytes 4194304 | tf_op jit(solution)/shard_map/all_to_all | solution.py:79
  186.2 7.0 %subtract_convert_fusion.1 = bf16[8,16,128,128]{3,2,1,0:T(8,128)(2,1)S(1)} fusion(f32[8,16,128,128]{3,2,1,0:T(8,128)} %get-tuple-element.102, f32[16,128,128]{2,1,0:T(8,128)S(1)} %get-tuple-element.83), kind=kOutput, calls=%fused_computation.3 | output fusion | flops 20971520 | bytes 13631488 | tf_op jit(solution)/shard_map/jit(cumsum)/reduce_window_sum | solution.py:46
  193.3 3.0 %fusion.9 = f32[8,16,128,64]{2,3,1,0:T(8,128)S(1)} fusion(bf16[8,16,128,128]{3,2,1,0:T(8,128)(2,1)S(1)} %subtract_convert_fusion.1, bf16[8,64,16,128]{3,2,1,0:T(8,128)(2,1)S(1)} %bitcast.75), kind=kOutput, calls=%fused_computation.21 | convolution fusion | flops 268435456 | bytes 10485760 | tf_op jit(solution)/shard_map/nche,nhde->nchd/dot_general | solution.py:62
  200.7 10.4 %all-to-all-done.2 = bf16[512,16,128]{2,1,0:T(8,128)(2,1)} async-done(((bf16[512,16,128]{2,1,0:T(8,128)(2,1)}), bf16[512,16,128]{2,1,0:T(8,128)(2,1)}, u32[]{:S(2)}, u32[]{:S(2)}) %all-to-all-start.2) | async-done | bytes 2097184 | tf_op jit(solution)/shard_map/all_to_all | solution.py:79
  211.1 5.3 %all-to-all-start = ((bf16[512,16,128]{2,1,0:T(8,128)(2,1)}), bf16[512,16,128]{2,1,0:T(8,128)(2,1)}, u32[]{:S(2)}, u32[]{:S(2)}) async-start(bf16[512,16,128]{2,1,0:T(8,128)(2,1)} %bitcast.82), calls=%async_computation | async-start | bytes 4194304 | tf_op jit(solution)/shard_map/all_to_all | solution.py:77
  223.9 3.6 %copy.104 = bf16[128,4,16,128]{3,2,1,0:T(8,128)(2,1)} copy(bf16[128,4,16,128]{3,2,0,1:T(8,128)(2,1)} %bitcast.21) | data formatting | bytes 4194304 | tf_op jit(solution)/shard_map/all_to_all | solution.py:78
  227.4 3.6 %copy.110 = bf16[128,4,16,128]{3,2,1,0:T(8,128)(2,1)} copy(bf16[128,4,16,128]{3,2,0,1:T(8,128)(2,1)} %bitcast.27) | data formatting | bytes 4194304 | tf_op jit(solution)/shard_map/all_to_all | solution.py:79
  231.0 10.3 %all-to-all-done = bf16[512,16,128]{2,1,0:T(8,128)(2,1)} async-done(((bf16[512,16,128]{2,1,0:T(8,128)(2,1)}), bf16[512,16,128]{2,1,0:T(8,128)(2,1)}, u32[]{:S(2)}, u32[]{:S(2)}) %all-to-all-start) | async-done | bytes 2097184 | tf_op jit(solution)/shard_map/all_to_all | solution.py:77
  241.3 3.6 %copy.94 = bf16[128,4,16,128]{3,2,1,0:T(8,128)(2,1)} copy(bf16[128,4,16,128]{3,2,0,1:T(8,128)(2,1)} %bitcast.14) | data formatting | bytes 4194304 | tf_op jit(solution)/shard_map/all_to_all | solution.py:77
  (54 shorter events, 27.6 us)
Async XLA Ops:
  7.2 9.4 %copy-start = (bf16[512,16,128]{2,1,0:T(8,128)(2,1)S(1)}, bf16[512,16,128]{2,1,0:T(8,128)(2,1)}, u32[]{:S(2)}) copy-start(bf16[512,16,128]{2,1,0:T(8,128)(2,1)} %param.10) | copy-start | bytes 6291460
  7.2 89.8 %all-gather.7.cloned.1.call-start = ((), (), s32[]{:S(2)}) async-start(), calls=%async_computation.4 | async-start | bytes 5242880 | tf_op jit(solution)/shard_map/all_gather | solution.py:13
  7.2 2.9 %copy-start.7 = (bf16[512,16,128]{2,1,0:T(8,128)(2,1)S(1)}, bf16[512,16,128]{2,1,0:T(8,128)(2,1)}, u32[]{:S(2)}) copy-start(bf16[512,16,128]{2,1,0:T(8,128)(2,1)} %param.11) | copy-start | bytes 6291460
  10.1 5.0 %copy-start.3 = (bf16[512,16,128]{2,1,0:T(8,128)(2,1)}, bf16[512,16,128]{2,1,0:T(8,128)(2,1)S(1)}, u32[]{:S(2)}) copy-start(bf16[512,16,128]{2,1,0:T(8,128)(2,1)S(1)} %multiply_convert_fusion) | copy-start | bytes 6291460
  16.5 161.4 %all-gather.5.cloned.1.call-start = ((), (), s32[]{:S(2)}) async-start(), calls=%async_computation.3 | async-start | bytes 5242880 | tf_op jit(solution)/shard_map/all_gather | solution.py:13
  32.5 4.3 %copy-start.4 = (bf16[512,16,128]{2,1,0:T(8,128)(2,1)S(1)}, bf16[512,16,128]{2,1,0:T(8,128)(2,1)}, u32[]{:S(2)}) copy-start(bf16[512,16,128]{2,1,0:T(8,128)(2,1)} %copy-done.3) | copy-start | bytes 6291460
  32.5 4.3 %copy-start.10 = (bf16[512,16,128]{2,1,0:T(8,128)(2,1)S(1)}, bf16[512,16,128]{2,1,0:T(8,128)(2,1)}, u32[]{:S(2)}) copy-start(bf16[512,16,128]{2,1,0:T(8,128)(2,1)} %param.9) | copy-start | bytes 6291460
  36.9 2.6 %copy-start.8 = (bf16[512,16,128]{2,1,0:T(8,128)(2,1)S(1)}, bf16[512,16,128]{2,1,0:T(8,128)(2,1)}, u32[]{:S(2)}) copy-start(bf16[512,16,128]{2,1,0:T(8,128)(2,1)} %param.11) | copy-start | bytes 6291460
  38.1 1.3 copy-start.14
  110.5 5.3 %copy-start.5 = (bf16[512,16,128]{2,1,0:T(8,128)(2,1)S(1)}, bf16[512,16,128]{2,1,0:T(8,128)(2,1)}, u32[]{:S(2)}) copy-start(bf16[512,16,128]{2,1,0:T(8,128)(2,1)} %copy-done.3) | copy-start | bytes 6291460
  110.5 5.3 %copy-start.12 = (bf16[8,16,64,64]{3,2,1,0:T(8,128)(2,1)S(1)}, bf16[8,16,64,64]{3,2,1,0:T(8,128)(2,1)}, u32[]{:S(2)}) copy-start(bf16[8,16,64,64]{3,2,1,0:T(8,128)(2,1)} %select_convert_fusion) | copy-start | bytes 3145732
  119.8 61.3 %all-to-all-start.1 = ((bf16[512,16,128]{2,1,0:T(8,128)(2,1)}), bf16[512,16,128]{2,1,0:T(8,128)(2,1)}, u32[]{:S(2)}, u32[]{:S(2)}) async-start(bf16[512,16,128]{2,1,0:T(8,128)(2,1)} %bitcast.81), calls=%async_computation.1 | async-start | bytes 4194304 | tf_op jit(solution)/shard_map/all_to_all | solution.py:78
  181.0 30.1 %all-to-all-start.2 = ((bf16[512,16,128]{2,1,0:T(8,128)(2,1)}), bf16[512,16,128]{2,1,0:T(8,128)(2,1)}, u32[]{:S(2)}, u32[]{:S(2)}) async-start(bf16[512,16,128]{2,1,0:T(8,128)(2,1)} %bitcast.80), calls=%async_computation.2 | async-start | bytes 4194304 | tf_op jit(solution)/shard_map/all_to_all | solution.py:79
  186.2 7.0 %copy-start.9 = (bf16[512,16,128]{2,1,0:T(8,128)(2,1)S(1)}, bf16[512,16,128]{2,1,0:T(8,128)(2,1)}, u32[]{:S(2)}) copy-start(bf16[512,16,128]{2,1,0:T(8,128)(2,1)} %param.11) | copy-start | bytes 6291460
  193.2 3.0 %copy-start.1 = (bf16[8,16,128,128]{3,2,1,0:T(8,128)(2,1)}, bf16[8,16,128,128]{3,2,1,0:T(8,128)(2,1)S(1)}, u32[]{:S(2)}) copy-start(bf16[8,16,128,128]{3,2,1,0:T(8,128)(2,1)S(1)} %subtract_convert_fusion.1) | copy-start | bytes 12582916
  193.2 3.1 %copy-start.11 = (bf16[512,16,128]{2,1,0:T(8,128)(2,1)S(1)}, bf16[512,16,128]{2,1,0:T(8,128)(2,1)}, u32[]{:S(2)}) copy-start(bf16[512,16,128]{2,1,0:T(8,128)(2,1)} %param.9) | copy-start | bytes 6291460
  193.3 3.7 %copy-start.13 = (bf16[8,16,64,64]{3,2,1,0:T(8,128)(2,1)S(1)}, bf16[8,16,64,64]{3,2,1,0:T(8,128)(2,1)}, u32[]{:S(2)}) copy-start(bf16[8,16,64,64]{3,2,1,0:T(8,128)(2,1)} %select_convert_fusion) | copy-start | bytes 3145732
  211.1 30.2 %all-to-all-start = ((bf16[512,16,128]{2,1,0:T(8,128)(2,1)}), bf16[512,16,128]{2,1,0:T(8,128)(2,1)}, u32[]{:S(2)}, u32[]{:S(2)}) async-start(bf16[512,16,128]{2,1,0:T(8,128)(2,1)} %bitcast.82), calls=%async_computation | async-start | bytes 4194304 | tf_op jit(solution)/shard_map/all_to_all | solution.py:77
  216.4 2.8 %copy-start.2 = (bf16[8,16,128,128]{3,2,1,0:T(8,128)(2,1)S(1)}, bf16[8,16,128,128]{3,2,1,0:T(8,128)(2,1)}, u32[]{:S(2)}) copy-start(bf16[8,16,128,128]{3,2,1,0:T(8,128)(2,1)} %copy-done.1) | copy-start | bytes 12582916
  216.4 3.5 %copy-start.6 = (bf16[512,16,128]{2,1,0:T(8,128)(2,1)S(1)}, bf16[512,16,128]{2,1,0:T(8,128)(2,1)}, u32[]{:S(2)}) copy-start(bf16[512,16,128]{2,1,0:T(8,128)(2,1)} %copy-done.3) | copy-start | bytes 6291460
Sparse Core Ops, SparseCore 0:
  16.6 80.3 all-gather.6
  98.6 79.2 all-gather.4
where the time goes:
time: 253 us; the launch traced here: 252 us
  waiting for transfers between devices  112 us (44%)
  matrix products  40.3 us (16%)
  local copies, waits for them, and re-layouts  36.1 us (14%)
  other arithmetic  33.1 us (13%)
  starting transfers between devices  15.7 us (6%)
  between operations  14.3 us (6%)
    all_gather x2, waiting for transfers between devices, prefix(): gathered = lax.all_gather(part, axis)  91.2 us
    all_to_all x1, waiting for transfers between devices, per_device(): lax.all_to_all(value_grad, ('head', 'sub'), split_axis=0, concat_axis=1,...  10.4 us
    convert_element_type x1, other arithmetic, per_device(): suffix_low = suffix.astype(jnp.bfloat16)  10.3 us
    all_to_all x1, waiting for transfers between devices, per_device(): lax.all_to_all(query_grad, ('head', 'sub'), split_axis=0, concat_axis=1,...  10.3 us
    rev x1, local copies, waits for them, and re-layouts, per_device(): suffix = after[None] + jnp.cumsum(adj_block[::-1], 0)[::-1] - adj_block  8.39 us
    another operation x1, other arithmetic, per_device(): suffix = after[None] + jnp.cumsum(adj_block[::-1], 0)[::-1] - adj_block  8.34 us
    dot_general x1, matrix products, per_device(): jnp.einsum('nchd,nche->nhde', kch, vch, preferred_element_type=jnp.float32)  7.57 us
    another operation x1, other arithmetic, per_device(): state = before[None] + jnp.cumsum(kv_block, 0) - kv_block  7.03 us
  transfers between devices with their start and end apart: 5, of which 4 were waited for; matrix products, arithmetic and copies ran while one was open for 37% of the time, Pallas kernels for 0%

commit v1 on v0

v1 whole, which is shorter than its diff:
```python
import functools

import jax
import jax.numpy as jnp
from jax import lax
from jax.experimental import pallas as pl
from jax.experimental.pallas import tpu as pltpu
from jax.sharding import PartitionSpec as P

MESH = pl.DeviceIdType.MESH
CHUNK = 128
GROUP = 2
F32 = jnp.float32
BF16 = jnp.bfloat16


def dot(a, b, da, db):
    return lax.dot_general(a, b, (((da,), (db,)), ((), ())), preferred_element_type=F32)


def main_kernel(
    nseq, nhead, nsub,
    k_hbm, v_hbm, d_hbm, q_hbm,
    att_out, qg_out, kg_out, vg_out,
    raw, kt, vt, dt, qt, fac, kv_loc, kv_tot, ad_loc, ad_tot,
    pre_in, pre_out, suf_in, suf_out, gq, gk, gv, att,
    in_sem, z_send, z_recv, x_send, x_recv, own_sem, att_sem,
):
    heads, tok, dim = kt.shape
    n = nhead * nsub
    tok_out = tok // n
    size = min(GROUP, heads)
    groups = heads // size
    chunks = tok // CHUNK
    seq = lax.axis_index("seq")
    sub = lax.axis_index("sub")
    me = lax.axis_index("head") * nsub + sub
    last = nseq - 1
    offsets = sorted(range(1, n), key=lambda o: -min(o, n - o))

    def mate(off):
        other = lax.rem(me + off, n)
        return other, {"head": other // nsub, "sub": lax.rem(other, nsub)}

    barrier = pltpu.get_barrier_semaphore()
    for off in offsets:
        pl.semaphore_signal(barrier, inc=1, device_id=mate(off)[1], device_id_type=MESH)

    @pl.when(seq > 0)
    def _():
        pl.semaphore_signal(barrier, inc=1, device_id={"seq": seq - 1}, device_id_type=MESH)

    @pl.when(seq < last)
    def _():
        pl.semaphore_signal(barrier, inc=1, device_id={"seq": seq + 1}, device_id_type=MESH)

    loads = [
        pltpu.make_async_copy(ref, raw.at[i], in_sem.at[i])
        for i, ref in enumerate((k_hbm, v_hbm, d_hbm, q_hbm))
    ]
    lower = seq < (nseq + 1) // 2

    @pl.when(lower)
    def _():
        for i in (0, 1, 2, 3):
            loads[i].start()

    @pl.when(jnp.logical_not(lower))
    def _():
        for i in (2, 3, 0, 1):
            loads[i].start()

    row = lax.broadcasted_iota(jnp.int32, (tok, dim), 0)
    fac[...] = lax.rsqrt(F32(dim) * (seq * tok + row + 1).astype(F32))

    @pl.when(seq == 0)
    def _():
        pre_in[...] = jnp.zeros_like(pre_in)

    @pl.when(seq == last)
    def _():
        suf_in[...] = jnp.zeros_like(suf_in)

    pl.semaphore_wait(
        barrier, n - 1 + (seq > 0).astype(jnp.int32) + (seq < last).astype(jnp.int32)
    )

    block = 64

    def turn(i, out, scale=False):
        loads[i].wait()

        def one(b, _):
            rows = pl.ds(pl.multiple_of(b * block, block), block)
            x = jnp.swapaxes(raw[i, rows], 0, 1)
            if scale:
                x = (x.astype(F32) * fac[rows][None]).astype(BF16)
            out[:, rows, :] = x
            return 0

        lax.fori_loop(0, tok // block, one, 0)

    def part(c):
        return pl.ds(c * CHUNK, CHUNK)

    def total_kv():
        def one(h, _):
            acc = jnp.zeros((dim, dim), F32)
            for c in range(chunks):
                kv_loc[h, c] = acc
                acc = acc + dot(kt[h, part(c)], vt[h, part(c)], 0, 0)
            kv_tot[h] = acc
            return 0

        lax.fori_loop(0, heads, one, 0)

    def total_ad():
        def one(h, _):
            acc = jnp.zeros((dim, dim), F32)
            for c in reversed(range(chunks)):
                ad_loc[h, c] = acc
                acc = acc + dot(dt[h, part(c)], qt[h, part(c)], 0, 0)
            ad_tot[h] = acc
            return 0

        lax.fori_loop(0, heads, one, 0)

    def group(g):
        return pl.ds(g * size, size)

    def chain(way, g):
        src, dst, to = (pre_out, pre_in, seq + 1) if way == 0 else (suf_out, suf_in, seq - 1)
        return pltpu.make_async_remote_copy(
            src_ref=src.at[group(g)],
            dst_ref=dst.at[group(g)],
            send_sem=z_send.at[way, g],
            recv_sem=z_recv.at[way, g],
            device_id={"seq": to},
            device_id_type=MESH,
        )

    def pass_on(way, g):
        src, dst, tot = (pre_out, pre_in, kv_tot) if way == 0 else (suf_out, suf_in, ad_tot)
        gets, gives = (seq > 0, seq < last) if way == 0 else (seq < last, seq > 0)

        @pl.when(gets)
        def _():
            chain(way, g).wait_recv()

        @pl.when(gives)
        def _():
            src[group(g)] = (dst[group(g)].astype(F32) + tot[group(g)]).astype(BF16)
            chain(way, g).start()

    grads = (gq, gk, gv)
    outs = (qg_out, kg_out, vg_out)

    def cross(a, g, off):
        other, ids = mate(off)
        return pltpu.make_async_remote_copy(
            src_ref=grads[a].at[group(g), pl.ds(pl.multiple_of(other * tok_out, tok_out), tok_out)],
            dst_ref=outs[a].at[me, group(g)],
            send_sem=x_send.at[a, g, other],
            recv_sem=x_recv.at[a, g, me],
            device_id=ids,
            device_id_type=MESH,
        )

    def cross_in(a, g, off):
        other, ids = mate(off)
        return pltpu.make_async_remote_copy(
            src_ref=grads[a].at[group(g), pl.ds(pl.multiple_of(other * tok_out, tok_out), tok_out)],
            dst_ref=outs[a].at[other, group(g)],
            send_sem=x_send.at[a, g, other],
            recv_sem=x_recv.at[a, g, other],
            device_id=ids,
            device_id_type=MESH,
        )

    def own(a, g):
        return pltpu.make_async_copy(
            grads[a].at[group(g), pl.ds(pl.multiple_of(me * tok_out, tok_out), tok_out)],
            outs[a].at[me, group(g)],
            own_sem.at[a, g],
        )

    def send(a, g):
        for off in offsets:
            cross(a, g, off).start()
        own(a, g).start()

    causal = lax.broadcasted_iota(jnp.int32, (CHUNK, CHUNK), 0) >= lax.broadcasted_iota(
        jnp.int32, (CHUNK, CHUNK), 1
    )

    def masked(a, b):
        return jnp.where(causal, dot(a, b, 1, 1), 0.0).astype(BF16)

    def loop_q():
        def one(g, _):
            pass_on(0, g)
            for i in range(size):
                h = g * size + i
                before = pre_in[h].astype(F32)
                for c in range(chunks):
                    state = (before + kv_loc[h, c]).astype(BF16)
                    d = dt[h, part(c)]
                    adj = masked(d, vt[h, part(c)])
                    out = dot(d, state, 1, 1) + dot(adj, kt[h, part(c)], 1, 0)
                    gq[h, part(c)] = (out * fac[part(c)]).astype(BF16)
            send(0, g)
            return 0

        lax.fori_loop(0, groups, one, 0)

    def loop_kv():
        def one(g, _):
            pass_on(1, g)
            for i in range(size):
                h = g * size + i
                after = suf_in[h].astype(F32)
                for c in range(chunks):
                    state = (after + ad_loc[h, c]).astype(BF16)
                    q, k, v, d = (x[h, part(c)] for x in (qt, kt, vt, dt))
                    adj = masked(d, v)
                    scores = masked(q, k)
                    gk[h, part(c)] = (dot(v, state, 1, 0) + dot(adj, q, 0, 0)).astype(BF16)
                    gv[h, part(c)] = (dot(k, state, 1, 1) + dot(scores, d, 0, 0)).astype(BF16)
            send(1, g)
            send(2, g)
            return 0

        lax.fori_loop(0, groups, one, 0)

    @pl.when(lower)
    def _():
        turn(0, kt)
        turn(1, vt)
        total_kv()
        turn(2, dt)
        loop_q()
        turn(3, qt, True)
        total_ad()
        loop_kv()

    @pl.when(jnp.logical_not(lower))
    def _():
        turn(2, dt)
        turn(3, qt, True)
        total_ad()
        turn(0, kt)
        turn(1, vt)
        loop_kv()
        total_kv()
        loop_q()

    def write(g):
        return pltpu.make_async_copy(att.at[group(g)], att_out.at[group(g)], att_sem.at[g])

    def attend(g, _):
        for i in range(size):
            h = g * size + i
            before = pre_in[h].astype(F32)
            for c in range(chunks):
                state = (before + kv_loc[h, c]).astype(BF16)
                q = qt[h, part(c)]
                scores = masked(q, kt[h, part(c)])
                out = dot(q, state, 1, 0) + dot(scores, vt[h, part(c)], 1, 0)
                att[h, part(c)] = out.astype(BF16)
        write(g).start()
        return 0

    lax.fori_loop(0, groups, attend, 0)

    def drain(g, _):
        @pl.when(seq < last)
        def _():
            chain(0, g).wait_send()

        @pl.when(seq > 0)
        def _():
            chain(1, g).wait_send()

        write(g).wait()
        for a in range(3):
            own(a, g).wait()
            for off in offsets:
                copy = cross_in(a, g, off)
                copy.wait_send()
                copy.wait_recv()
        return 0

    lax.fori_loop(0, groups, drain, 0)


def exchange(nseq, nhead, nsub, queries, key_rows, value_rows, out_adjoint):
    tok, heads, dim = queries.shape
    n = nhead * nsub
    chunks = tok // CHUNK
    groups = heads // min(GROUP, heads)
    turned = pltpu.VMEM((heads, tok, dim), BF16)
    low = pltpu.VMEM((heads, dim, dim), BF16)
    any_spec = pl.BlockSpec(memory_space=pl.ANY)
    grad = jax.ShapeDtypeStruct((n, heads, tok // n, dim), BF16)
    return pl.pallas_call(
        functools.partial(main_kernel, nseq, nhead, nsub),
        out_shape=(jax.ShapeDtypeStruct((heads, tok, dim), BF16), grad, grad, grad),
        in_specs=[any_spec] * 4,
        out_specs=(any_spec,) * 4,
        scratch_shapes=[
            pltpu.VMEM((4, tok, heads, dim), BF16),
            turned, turned, turned, turned,
            pltpu.VMEM((tok, dim), F32),
            pltpu.VMEM((heads, chunks, dim, dim), F32),
            pltpu.VMEM((heads, dim, dim), F32),
            pltpu.VMEM((heads, chunks, dim, dim), F32),
            pltpu.VMEM((heads, dim, dim), F32),
            low, low, low, low,
            turned, turned, turned, turned,
            pltpu.SemaphoreType.DMA((4,)),
            pltpu.SemaphoreType.DMA((2, groups)),
            pltpu.SemaphoreType.DMA((2, groups)),
            pltpu.SemaphoreType.DMA((3, groups, n)),
            pltpu.SemaphoreType.DMA((3, groups, n)),
            pltpu.SemaphoreType.DMA((3, groups)),
            pltpu.SemaphoreType.DMA((groups,)),
        ],
        compiler_params=pltpu.CompilerParams(
            collective_id=0, has_side_effects=True, vmem_limit_bytes=50 * 2**20
        ),
    )(key_rows, value_rows, out_adjoint, queries)


def finish_kernel(att, a, b, c, att_out, a_out, b_out, c_out):
    att_out[...] = jnp.swapaxes(att[...], 0, 1)
    for src, dst in ((a, a_out), (b, b_out), (c, c_out)):
        n, heads, rows, dim = src.shape
        dst[...] = jnp.swapaxes(src[...].reshape(n * heads, rows, dim), 0, 1)


def finish(att, *grads):
    heads, tok, dim = att.shape
    n, _, rows, _ = grads[0].shape
    steps = max(1, rows // 16)
    tb, rb = tok // steps, rows // steps
    return pl.pallas_call(
        finish_kernel,
        grid=(steps,),
        out_shape=(jax.ShapeDtypeStruct((tok, heads, dim), BF16),)
        + (jax.ShapeDtypeStruct((rows, n * heads, dim), BF16),) * 3,
        in_specs=[pl.BlockSpec((heads, tb, dim), lambda i: (0, i, 0))]
        + [pl.BlockSpec((n, heads, rb, dim), lambda i: (0, 0, i, 0))] * 3,
        out_specs=(pl.BlockSpec((tb, heads, dim), lambda i: (i, 0, 0)),)
        + (pl.BlockSpec((rb, n * heads, dim), lambda i: (i, 0, 0)),) * 3,
        compiler_params=pltpu.CompilerParams(vmem_limit_bytes=32 * 2**20),
    )(att, *grads)


def solution(mesh):
    spec = P(("grp", "seq"), ("head", "sub"), None)
    grad = P(("grp", "seq", "head", "sub"), None, None)

    def per_device(queries, key_rows, value_rows, out_adjoint):
        return finish(
            *exchange(
                mesh.shape["seq"], mesh.shape["head"], mesh.shape["sub"],
                queries, key_rows, value_rows, out_adjoint,
            )
        )

    return jax.shard_map(
        per_device, mesh=mesh, in_specs=(spec,) * 4, out_specs=(spec, grad, grad, grad),
        check_vma=False,
    )
```

time: 253 us -> 96.2 us (0.38)
  waiting for transfers between devices: 112 us -> 0 us
  Pallas kernels: 0 us -> 90.6 us
  matrix products: 40.3 us -> 0 us
  other arithmetic: 33.1 us -> 0 us
  local copies, waits for them, and re-layouts: 36.1 us -> 4.77 us
  starting transfers between devices: 15.7 us -> 0 us
  between operations: 14.3 us -> 0.65 us
    all_gather x2 -> x0, waiting for transfers between devices: 91.2 us -> none  [prefix(): gathered = lax.all_gather(part, axis)]
    pallas_call x0 -> x2, Pallas kernels: none -> 90.6 us  [the longest x1 85.2 us: exchange(): pl.pallas_call(functools.partial(main_kernel, nseq, nhead, nsub), out_sha...]
    dot_general x12 -> x0, matrix products: 40.3 us -> none  [the longest x1 7.57 us: per_device(): jnp.einsum('nchd,nche->nhde', kch, vch, preferred_element_type=jnp.float32)]
    all_to_all x3 -> x0, waiting for transfers between devices: 20.7 us -> none  [the longest x1 10.4 us: per_device(): lax.all_to_all(value_grad, ('head', 'sub'), split_axis=0, concat_axis=1,...]
    all_to_all x3 -> x0, starting transfers between devices: 15.7 us -> none  [the longest x1 5.27 us: per_device(): lax.all_to_all(query_grad, ('head', 'sub'), split_axis=0, concat_axis=1,...]
    another operation x2 -> x0, other arithmetic: 15.4 us -> none  [the longest x1 8.34 us: per_device(): suffix = after[None] + jnp.cumsum(adj_block[::-1], 0)[::-1] - adj_block]
    convert_element_type x2 -> x0, other arithmetic: 13.2 us -> none  [the longest x1 10.3 us: per_device(): suffix_low = suffix.astype(jnp.bfloat16)]
    convert_element_type x4 -> x0, local copies, waits for them, and re-layouts: 11 us -> none  [the longest x1 2.77 us: per_device(): value_grad = value_grad.reshape(shape).astype(jnp.bfloat16)]
  transfers between devices with their start and end apart: 5 -> 0, of which waited for: 4 -> 0; matrix products, arithmetic and copies ran while one was open for 37% -> 0% of each run, Pallas kernels for 0% -> 0%
where the time goes in v1:
time: 96.2 us; the launch traced here: 96 us
  Pallas kernels  90.6 us (94%)
  local copies, waits for them, and re-layouts  4.77 us (5%)
    pallas_call x1, Pallas kernels, exchange(): pl.pallas_call(functools.partial(main_kernel, nseq, nhead, nsub), out_sha...  85.2 us
    pallas_call x1, Pallas kernels, finish(): pl.pallas_call(finish_kernel, grid=(steps,), out_shape=(jax.ShapeDtypeStr...  5.39 us
    unnamed x6, local copies, waits for them, and re-layouts  4.77 us

profile of v1, /device:TPU:17, one launch (start us, length us, event | category | flops | bytes accessed | tf_op | source)
XLA Modules:
  0.0 96.0 jit_solution(4429425117645477042)
XLA Ops:
  0.6 85.2 %shard_map.75 = (bf16[16,512,128]{2,1,0:T(8,128)(2,1)S(1)}, bf16[4,16,128,128]{3,2,1,0:T(8,128)(2,1)}, bf16[4,16,128,128]{3,2,1,0:T(8,128)(2,1)}, bf16[4,16,128,128]{3,2,1,0:T(8,128)(2,1)}) custom-call(bf16[512,16,128]{2,1,0:T(8,128)(2,1)} %k_hbm.1, bf16[512,16,128]{2,1,0:T(8,128)(2,1)} %v_hbm.1, bf16[512,16,128]{2,1,0:T(8,128)(2,1)} %d_hbm.1, ...), custom_call_target="tpu_custom_call" | custom-call | tf_op jit(solution)/shard_map/pallas_call | solution.py:305
  85.9 0.0 copy-start
  85.9 1.6 %copy-done = bf16[4,16,128,128]{3,2,1,0:T(8,128)(2,1)S(1)} copy-done((bf16[4,16,128,128]{3,2,1,0:T(8,128)(2,1)S(1)}, bf16[4,16,128,128]{3,2,1,0:T(8,128)(2,1)}, u32[]{:S(2)}) %copy-start) | copy-done | bytes 2097176
  87.5 0.0 copy-start.1
  87.5 1.6 %copy-done.1 = bf16[4,16,128,128]{3,2,1,0:T(8,128)(2,1)S(1)} copy-done((bf16[4,16,128,128]{3,2,1,0:T(8,128)(2,1)S(1)}, bf16[4,16,128,128]{3,2,1,0:T(8,128)(2,1)}, u32[]{:S(2)}) %copy-start.1) | copy-done | bytes 2097176
  89.0 0.0 copy-start.2
  89.0 1.6 %copy-done.2 = bf16[4,16,128,128]{3,2,1,0:T(8,128)(2,1)S(1)} copy-done((bf16[4,16,128,128]{3,2,1,0:T(8,128)(2,1)S(1)}, bf16[4,16,128,128]{3,2,1,0:T(8,128)(2,1)}, u32[]{:S(2)}) %copy-start.2) | copy-done | bytes 2097176
  90.6 5.4 %shard_map.76 = (bf16[512,16,128]{2,1,0:T(8,128)(2,1)}, bf16[128,64,128]{2,1,0:T(8,128)(2,1)}, bf16[128,64,128]{2,1,0:T(8,128)(2,1)}, bf16[128,64,128]{2,1,0:T(8,128)(2,1)}) custom-call(bf16[16,512,128]{2,1,0:T(8,128)(2,1)S(1)} %get-tuple-element.8.att, bf16[4,16,128,128]{3,2,1,0:T(8,128)(2,1)S(1)} %copy-done, bf16[4,16,128,128]{3,2,1,0:T(8,128)(2,1)S(1)} %copy-done.1, ...), custom_call_target="tpu_custom_call" | custom-call | tf_op jit(solution)/shard_map/pallas_call | solution.py:346
Async XLA Ops:
  85.9 1.6 %copy-start = (bf16[4,16,128,128]{3,2,1,0:T(8,128)(2,1)S(1)}, bf16[4,16,128,128]{3,2,1,0:T(8,128)(2,1)}, u32[]{:S(2)}) copy-start(bf16[4,16,128,128]{3,2,1,0:T(8,128)(2,1)} %get-tuple-element.9.a) | copy-start | bytes 6291460
  87.5 1.6 %copy-start.1 = (bf16[4,16,128,128]{3,2,1,0:T(8,128)(2,1)S(1)}, bf16[4,16,128,128]{3,2,1,0:T(8,128)(2,1)}, u32[]{:S(2)}) copy-start(bf16[4,16,128,128]{3,2,1,0:T(8,128)(2,1)} %get-tuple-element.10.b) | copy-start | bytes 6291460
  89.0 1.6 %copy-start.2 = (bf16[4,16,128,128]{3,2,1,0:T(8,128)(2,1)S(1)}, bf16[4,16,128,128]{3,2,1,0:T(8,128)(2,1)}, u32[]{:S(2)}) copy-start(bf16[4,16,128,128]{3,2,1,0:T(8,128)(2,1)} %get-tuple-element.11.c) | copy-start | bytes 6291460

commit v2 on v1

v2 whole, which is shorter than its diff:
```python
import functools

import jax
import jax.numpy as jnp
from jax import lax
from jax.experimental import pallas as pl
from jax.experimental.pallas import tpu as pltpu
from jax.sharding import PartitionSpec as P

MESH = pl.DeviceIdType.MESH
CHUNK = 128
GROUP = 2
F32 = jnp.float32
BF16 = jnp.bfloat16


def dot(a, b, da, db):
    return lax.dot_general(a, b, (((da,), (db,)), ((), ())), preferred_element_type=F32)


def main_kernel(
    nseq, nhead, nsub,
    k_hbm, v_hbm, d_hbm, q_hbm,
    att_out, grad_out,
    raw, kt, vt, dt, qt, fac, kv_loc, kv_tot, ad_loc, ad_tot,
    pre_in, pre_out, suf_in, suf_out, grads, held, stage, att,
    in_sem, z_send, z_recv, x_send, x_recv, own_sem, att_sem, out_sem,
):
    heads, tok, dim = kt.shape
    n = nhead * nsub
    tok_out = tok // n
    size = min(GROUP, heads)
    groups = heads // size
    chunks = tok // CHUNK
    seq = lax.axis_index("seq")
    me = lax.axis_index("head") * nsub + lax.axis_index("sub")
    last = nseq - 1
    offsets = sorted(range(1, n), key=lambda o: -min(o, n - o))

    def mate(off):
        other = lax.rem(me + off, n)
        return other, {"head": other // nsub, "sub": lax.rem(other, nsub)}

    barrier = pltpu.get_barrier_semaphore()
    for off in offsets:
        pl.semaphore_signal(barrier, inc=1, device_id=mate(off)[1], device_id_type=MESH)

    @pl.when(seq > 0)
    def _():
        pl.semaphore_signal(barrier, inc=1, device_id={"seq": seq - 1}, device_id_type=MESH)

    @pl.when(seq < last)
    def _():
        pl.semaphore_signal(barrier, inc=1, device_id={"seq": seq + 1}, device_id_type=MESH)

    lower = seq < (nseq + 1) // 2
    upper = jnp.logical_not(lower)
    sources = (k_hbm, v_hbm, d_hbm, q_hbm)

    def load(i, c):
        rows = pl.ds(pl.multiple_of(c * CHUNK, CHUNK), CHUNK)
        return pltpu.make_async_copy(sources[i].at[rows], raw.at[i, rows], in_sem.at[i, c])

    def load_all(order):
        for i in order:
            for c in range(chunks):
                load(i, c).start()

    @pl.when(lower)
    def _():
        load_all((0, 1, 2, 3))

    @pl.when(upper)
    def _():
        load_all((2, 3, 1, 0))

    row = lax.broadcasted_iota(jnp.int32, (tok, dim), 0)
    fac[...] = lax.rsqrt(F32(dim) * (seq * tok + row + 1).astype(F32))

    @pl.when(seq == 0)
    def _():
        pre_in[...] = jnp.zeros_like(pre_in)

    @pl.when(seq == last)
    def _():
        suf_in[...] = jnp.zeros_like(suf_in)

    block = 64

    def turn(i, out, scale=False):
        def one(c, _):
            load(i, c).wait()
            for b in range(CHUNK // block):
                rows = pl.ds(pl.multiple_of(c * CHUNK + b * block, block), block)
                x = jnp.swapaxes(raw[i, rows], 0, 1)
                if scale:
                    x = (x.astype(F32) * fac[rows][None]).astype(BF16)
                out[:, rows, :] = x
            return 0

        lax.fori_loop(0, chunks, one, 0)

    def part(c):
        return pl.ds(c * CHUNK, CHUNK)

    def group(g):
        return pl.ds(g * size, size)

    def chain(way, g):
        src, dst, to = (pre_out, pre_in, seq + 1) if way == 0 else (suf_out, suf_in, seq - 1)
        return pltpu.make_async_remote_copy(
            src_ref=src.at[group(g)],
            dst_ref=dst.at[group(g)],
            send_sem=z_send.at[way, g],
            recv_sem=z_recv.at[way, g],
            device_id={"seq": to},
            device_id_type=MESH,
        )

    def ends(way):
        return (seq > 0, seq < last) if way == 0 else (seq < last, seq > 0)

    def total(way, g):
        left, right, loc, tot, out = (
            (kt, vt, kv_loc, kv_tot, pre_out) if way == 0 else (dt, qt, ad_loc, ad_tot, suf_out)
        )
        for i in range(size):
            h = g * size + i
            acc = jnp.zeros((dim, dim), F32)
            for c in range(chunks) if way == 0 else reversed(range(chunks)):
                loc[h, c] = acc
                acc = acc + dot(left[h, part(c)], right[h, part(c)], 0, 0)
            tot[h] = acc
        gets, gives = ends(way)

        @pl.when(jnp.logical_and(jnp.logical_not(gets), gives))
        def _():
            out[group(g)] = tot[group(g)].astype(BF16)
            chain(way, g).start()

    def pass_on(way, g):
        src, dst, tot = (pre_out, pre_in, kv_tot) if way == 0 else (suf_out, suf_in, ad_tot)
        gets, gives = ends(way)

        @pl.when(gets)
        def _():
            chain(way, g).wait_recv()

        @pl.when(jnp.logical_and(gets, gives))
        def _():
            src[group(g)] = (dst[group(g)].astype(F32) + tot[group(g)]).astype(BF16)
            chain(way, g).start()

    def mine(a, g, other):
        rows = pl.ds(pl.multiple_of(other * tok_out, tok_out), tok_out)
        return grads.at[a, group(g), rows]

    def cross(a, g, off, arriving=False):
        other, ids = mate(off)
        src = other if arriving else me
        return pltpu.make_async_remote_copy(
            src_ref=mine(a, g, other),
            dst_ref=held.at[a, src, group(g)],
            send_sem=x_send.at[a, g, other],
            recv_sem=x_recv.at[a, g, src],
            device_id=ids,
            device_id_type=MESH,
        )

    def own(a, g):
        return pltpu.make_async_copy(mine(a, g, me), held.at[a, me, group(g)], own_sem.at[a, g])

    def send(a, g):
        for off in offsets:
            cross(a, g, off).start()
        own(a, g).start()

    across = lax.broadcasted_iota(jnp.int32, (CHUNK, CHUNK), 0)
    along = lax.broadcasted_iota(jnp.int32, (CHUNK, CHUNK), 1)

    def masked(a, b):
        return jnp.where(across >= along, dot(a, b, 1, 1), 0.0).astype(BF16)

    def masked_t(a, b):
        return jnp.where(across <= along, dot(a, b, 1, 1), 0.0).astype(BF16)

    def walk(way, a, first, compute):
        if first:
            total(way, 0)

        def one(g, _):
            if first:
                @pl.when(g + 1 < groups)
                def _():
                    total(way, g + 1)

                pass_on(way, g)
            edge, loc = (pre_in, kv_loc) if way == 0 else (suf_in, ad_loc)
            for i in range(size):
                h = g * size + i
                outer = edge[h].astype(F32)
                for c in range(chunks):
                    state = (outer + loc[h, c]).astype(BF16)
                    grads[a, h, part(c)] = compute(h, c, state).astype(BF16)
            send(a, g)
            return 0

        lax.fori_loop(0, groups, one, 0)

    def query_part(h, c, state):
        d = dt[h, part(c)]
        adj = masked(d, vt[h, part(c)])
        return (dot(d, state, 1, 1) + dot(adj, kt[h, part(c)], 1, 0)) * fac[part(c)]

    def key_part(h, c, state):
        v = vt[h, part(c)]
        adj = masked_t(v, dt[h, part(c)])
        return dot(v, state, 1, 0) + dot(adj, qt[h, part(c)], 1, 0)

    def value_part(h, c, state):
        k = kt[h, part(c)]
        scores = masked_t(k, qt[h, part(c)])
        return dot(k, state, 1, 1) + dot(scores, dt[h, part(c)], 1, 0)

    @pl.when(lower)
    def _():
        turn(0, kt)
        turn(1, vt)
        turn(2, dt)

    @pl.when(upper)
    def _():
        turn(2, dt)
        turn(3, qt, True)
        turn(1, vt)

    pl.semaphore_wait(
        barrier, n - 1 + (seq > 0).astype(jnp.int32) + (seq < last).astype(jnp.int32)
    )

    @pl.when(lower)
    def _():
        walk(0, 0, True, query_part)
        turn(3, qt, True)
        walk(1, 1, True, key_part)
        walk(1, 2, False, value_part)

    @pl.when(upper)
    def _():
        walk(1, 1, True, key_part)
        turn(0, kt)
        walk(1, 2, False, value_part)
        walk(0, 0, True, query_part)

    def attend(g, _):
        for i in range(size):
            h = g * size + i
            before = pre_in[h].astype(F32)
            for c in range(chunks):
                state = (before + kv_loc[h, c]).astype(BF16)
                q = qt[h, part(c)]
                scores = masked(q, kt[h, part(c)])
                out = dot(q, state, 1, 0) + dot(scores, vt[h, part(c)], 1, 0)
                att[h, part(c)] = out.astype(BF16)
        return 0

    lax.fori_loop(0, groups, attend, 0)

    def turn_att(c, _):
        rows = pl.ds(pl.multiple_of(c * block, block), block)
        raw[0, rows] = jnp.swapaxes(att[:, rows, :], 0, 1)
        return 0

    lax.fori_loop(0, tok // block, turn_att, 0)
    att_copy = pltpu.make_async_copy(raw.at[0], att_out, att_sem)
    att_copy.start()

    strip = min(16, tok_out)
    strips = tok_out // strip

    def put(a, slot, r):
        rows = pl.ds(pl.multiple_of(r * strip, strip), strip)
        return pltpu.make_async_copy(
            stage.at[slot, rows], grad_out.at[a, rows], out_sem.at[slot, r]
        )

    def gather(i, _):
        a = lax.rem(i + upper.astype(jnp.int32), 3)
        slot = lax.rem(i, 2)

        def arrive(g, _):
            own(a, g).wait()
            for off in offsets:
                cross(a, g, off, True).wait_recv()
            return 0

        lax.fori_loop(0, groups, arrive, 0)

        @pl.when(i >= 2)
        def _():
            for r in range(strips):
                put(a, slot, r).wait()

        def one(r, _):
            rows = pl.ds(pl.multiple_of(r * strip, strip), strip)
            x = held[a, :, :, rows, :].reshape(n * heads, strip, dim)
            stage[slot, rows] = jnp.swapaxes(x, 0, 1)
            put(a, slot, r).start()
            return 0

        lax.fori_loop(0, strips, one, 0)
        return 0

    lax.fori_loop(0, 3, gather, 0)

    def drain(g, _):
        @pl.when(seq < last)
        def _():
            chain(0, g).wait_send()

        @pl.when(seq > 0)
        def _():
            chain(1, g).wait_send()

        for a in range(3):
            for off in offsets:
                cross(a, g, off).wait_send()
        return 0

    lax.fori_loop(0, groups, drain, 0)
    for slot in range(2):
        for r in range(strips):
            put(0, slot, r).wait()
    att_copy.wait()


def exchange(nseq, nhead, nsub, queries, key_rows, value_rows, out_adjoint):
    tok, heads, dim = queries.shape
    n = nhead * nsub
    tok_out = tok // n
    chunks = tok // CHUNK
    groups = heads // min(GROUP, heads)
    turned = pltpu.VMEM((heads, tok, dim), BF16)
    low = pltpu.VMEM((heads, dim, dim), BF16)
    any_spec = pl.BlockSpec(memory_space=pl.ANY)
    return pl.pallas_call(
        functools.partial(main_kernel, nseq, nhead, nsub),
        out_shape=(
            pltpu.VMEM((tok, heads, dim), BF16),
            pltpu.VMEM((3, tok_out, n * heads, dim), BF16),
        ),
        in_specs=[any_spec] * 4,
        out_specs=(any_spec,) * 2,
        scratch_shapes=[
            pltpu.VMEM((4, tok, heads, dim), BF16),
            turned, turned, turned, turned,
            pltpu.VMEM((tok, dim), F32),
            pltpu.VMEM((heads, chunks, dim, dim), F32),
            pltpu.VMEM((heads, dim, dim), F32),
            pltpu.VMEM((heads, chunks, dim, dim), F32),
            pltpu.VMEM((heads, dim, dim), F32),
            low, low, low, low,
            pltpu.VMEM((3, heads, tok, dim), BF16),
            pltpu.VMEM((3, n, heads, tok_out, dim), BF16),
            pltpu.VMEM((2, tok_out, n * heads, dim), BF16),
            turned,
            pltpu.SemaphoreType.DMA((4, chunks)),
            pltpu.SemaphoreType.DMA((2, groups)),
            pltpu.SemaphoreType.DMA((2, groups)),
            pltpu.SemaphoreType.DMA((3, groups, n)),
            pltpu.SemaphoreType.DMA((3, groups, n)),
            pltpu.SemaphoreType.DMA((3, groups)),
            pltpu.SemaphoreType.DMA,
            pltpu.SemaphoreType.DMA((2, tok_out // min(16, tok_out))),
        ],
        compiler_params=pltpu.CompilerParams(
            collective_id=0, has_side_effects=True, vmem_limit_bytes=50 * 2**20
        ),
    )(key_rows, value_rows, out_adjoint, queries)


def finish_kernel(pieces, att, grads, att_out, a_out, b_out, c_out, sem):
    outs = (att_out, a_out, b_out, c_out)
    copies = []
    for i, dst in enumerate(outs):
        src = att if i == 0 else grads.at[i - 1]
        step = dst.shape[0] // pieces
        for p in range(pieces):
            rows = pl.ds(p * step, step)
            copies.append(pltpu.make_async_copy(src.at[rows], dst.at[rows], sem.at[i, p]))
    for copy in copies:
        copy.start()
    for copy in copies:
        copy.wait()


def finish(att, grads):
    pieces = 4
    any_spec = pl.BlockSpec(memory_space=pl.ANY)
    return pl.pallas_call(
        functools.partial(finish_kernel, pieces),
        out_shape=(jax.ShapeDtypeStruct(att.shape, BF16),)
        + (jax.ShapeDtypeStruct(grads.shape[1:], BF16),) * 3,
        in_specs=[any_spec] * 2,
        out_specs=(any_spec,) * 4,
        scratch_shapes=[pltpu.SemaphoreType.DMA((4, pieces))],
        compiler_params=pltpu.CompilerParams(vmem_limit_bytes=2**20),
    )(att, grads)


def solution(mesh):
    spec = P(("grp", "seq"), ("head", "sub"), None)
    grad = P(("grp", "seq", "head", "sub"), None, None)

    def per_device(queries, key_rows, value_rows, out_adjoint):
        return finish(
            *exchange(
                mesh.shape["seq"], mesh.shape["head"], mesh.shape["sub"],
                queries, key_rows, value_rows, out_adjoint,
            )
        )

    return jax.shard_map(
        per_device, mesh=mesh, in_specs=(spec,) * 4, out_specs=(spec, grad, grad, grad),
        check_vma=False,
    )
```

time: 96.2 us -> 85.3 us (0.89)
  Pallas kernels: 90.6 us -> 84.5 us
  local copies, waits for them, and re-layouts: 4.77 us -> 0 us
    unnamed x6 -> x0, local copies, waits for them, and re-layouts: 4.77 us -> none
    pallas_call x1, Pallas kernels: 85.2 us -> 81.1 us  [exchange(): pl.pallas_call(functools.partial(main_kernel, nseq, nhead, nsub), out_sha...]
    pallas_call x1, Pallas kernels: 5.39 us -> 3.42 us  [finish(): pl.pallas_call(functools.partial(finish_kernel, pieces), out_shape=(jax.S...]
where the time goes in v2:
time: 85.3 us; the launch traced here: 85.1 us
  Pallas kernels  84.5 us (99%)
    pallas_call x1, Pallas kernels, exchange(): pl.pallas_call(functools.partial(main_kernel, nseq, nhead, nsub), out_sha...  81.1 us
    pallas_call x1, Pallas kernels, finish(): pl.pallas_call(functools.partial(finish_kernel, pieces), out_shape=(jax.S...  3.42 us

profile of v2, /device:TPU:17, one launch (start us, length us, event | category | flops | bytes accessed | tf_op | source)
XLA Modules:
  0.0 85.1 jit_solution(11446031238569347400)
XLA Ops:
  0.6 81.1 %shard_map.75 = (bf16[512,16,128]{2,1,0:T(8,128)(2,1)S(1)}, bf16[3,128,64,128]{3,2,1,0:T(8,128)(2,1)S(1)}) custom-call(bf16[512,16,128]{2,1,0:T(8,128)(2,1)} %k_hbm.1, bf16[512,16,128]{2,1,0:T(8,128)(2,1)} %v_hbm.1, bf16[512,16,128]{2,1,0:T(8,128)(2,1)} %d_hbm.1, bf16[512,16,128]{2,1,0:T(8,128)(2,1)} %q_hbm.1), custom_call_target="tpu_custom_call" | custom-call | tf_op jit(solution)/shard_map/pallas_call | solution.py:346
  81.7 3.4 %shard_map.76 = (bf16[512,16,128]{2,1,0:T(8,128)(2,1)}, bf16[128,64,128]{2,1,0:T(8,128)(2,1)}, bf16[128,64,128]{2,1,0:T(8,128)(2,1)}, bf16[128,64,128]{2,1,0:T(8,128)(2,1)}) custom-call(bf16[512,16,128]{2,1,0:T(8,128)(2,1)S(1)} %get-tuple-element.6.att, bf16[3,128,64,128]{3,2,1,0:T(8,128)(2,1)S(1)} %get-tuple-element.7.grads), custom_call_target="tpu_custom_call" | custom-call | tf_op jit(solution)/shard_map/pallas_call | solution.py:400

commit v3 on v2

--- a/solution.py
+++ b/solution.py
@@ -87,15 +87,25 @@
 
     block = 64
 
-    def turn(i, out, scale=False):
+    halves = 2 if heads % 16 == 0 else 1
+    half = heads // halves
+    half_groups = groups // halves
+
+    def some(p):
+        return pl.ds(p * half, half)
+
+    def turn(i, p, wait=False):
+        out = (kt, vt, dt, qt)[i]
+
         def one(c, _):
-            load(i, c).wait()
+            if wait:
+                load(i, c).wait()
             for b in range(CHUNK // block):
                 rows = pl.ds(pl.multiple_of(c * CHUNK + b * block, block), block)
-                x = jnp.swapaxes(raw[i, rows], 0, 1)
-                if scale:
+                x = jnp.swapaxes(raw[i, rows, some(p), :], 0, 1)
+                if i == 3:
                     x = (x.astype(F32) * fac[rows][None]).astype(BF16)
-                out[:, rows, :] = x
+                out[some(p), rows, :] = x
             return 0
 
         lax.fori_loop(0, chunks, one, 0)
@@ -184,13 +194,10 @@
     def masked_t(a, b):
         return jnp.where(across <= along, dot(a, b, 1, 1), 0.0).astype(BF16)
 
-    def walk(way, a, first, compute):
-        if first:
-            total(way, 0)
-
+    def walk(way, a, compute, begin, end, first):
         def one(g, _):
             if first:
-                @pl.when(g + 1 < groups)
+                @pl.when(g + 1 < end)
                 def _():
                     total(way, g + 1)
 
@@ -205,7 +212,12 @@
             send(a, g)
             return 0
 
-        lax.fori_loop(0, groups, one, 0)
+        lax.fori_loop(begin, end, one, 0)
+
+    def walk_all(way, a, compute, first):
+        if first:
+            total(way, 0)
+        walk(way, a, compute, 0, groups, first)
 
     def query_part(h, c, state):
         d = dt[h, part(c)]
@@ -224,33 +236,44 @@
 
     @pl.when(lower)
     def _():
-        turn(0, kt)
-        turn(1, vt)
-        turn(2, dt)
+        turn(0, 0, True)
+        turn(1, 0, True)
 
     @pl.when(upper)
     def _():
-        turn(2, dt)
-        turn(3, qt, True)
-        turn(1, vt)
+        turn(2, 0, True)
+        turn(3, 0, True)
 
     pl.semaphore_wait(
         barrier, n - 1 + (seq > 0).astype(jnp.int32) + (seq < last).astype(jnp.int32)
     )
 
+    def open_walk(way, a, compute, pair, third):
+        for p in range(halves):
+            if p:
+                for i in pair:
+                    turn(i, p)
+            total(way, p * half_groups)
+            turn(third, p, p == 0)
+            walk(way, a, compute, p * half_groups, (p + 1) * half_groups, True)
+
+    def turn_whole(i):
+        for p in range(halves):
+            turn(i, p, p == 0)
+
     @pl.when(lower)
     def _():
-        walk(0, 0, True, query_part)
-        turn(3, qt, True)
-        walk(1, 1, True, key_part)
-        walk(1, 2, False, value_part)
+        open_walk(0, 0, query_part, (0, 1), 2)
+        turn_whole(3)
+        walk_all(1, 1, key_part, True)
+        walk_all(1, 2, value_part, False)
 
     @pl.when(upper)
     def _():
-        walk(1, 1, True, key_part)
-        turn(0, kt)
-        walk(1, 2, False, value_part)
-        walk(0, 0, True, query_part)
+        open_walk(1, 1, key_part, (2, 3), 1)
+        turn_whole(0)
+        walk_all(1, 2, value_part, False)
+        walk_all(0, 0, query_part, True)
 
     def attend(g, _):
         for i in range(size):
@@ -288,27 +311,34 @@
         a = lax.rem(i + upper.astype(jnp.int32), 3)
         slot = lax.rem(i, 2)
 
+        @pl.when(i >= 2)
+        def _():
+            for r in range(strips):
+                put(a, slot, r).wait()
+
         def arrive(g, _):
             own(a, g).wait()
             for off in offsets:
                 cross(a, g, off, True).wait_recv()
             return 0
 
-        lax.fori_loop(0, groups, arrive, 0)
-
-        @pl.when(i >= 2)
-        def _():
-            for r in range(strips):
-                put(a, slot, r).wait()
-
-        def one(r, _):
-            rows = pl.ds(pl.multiple_of(r * strip, strip), strip)
-            x = held[a, :, :, rows, :].reshape(n * heads, strip, dim)
-            stage[slot, rows] = jnp.swapaxes(x, 0, 1)
-            put(a, slot, r).start()
-            return 0
-
-        lax.fori_loop(0, strips, one, 0)
+        for p in range(halves):
+            lax.fori_loop(p * half_groups, (p + 1) * half_groups, arrive, 0)
+
+            def one(r, _):
+                rows = pl.ds(pl.multiple_of(r * strip, strip), strip)
+                if halves == 1:
+                    x = held[a, :, :, rows, :].reshape(n * heads, strip, dim)
+                    stage[slot, rows] = jnp.swapaxes(x, 0, 1)
+                else:
+                    for src in range(n):
+                        x = jnp.swapaxes(held[a, src, some(p), rows, :], 0, 1)
+                        stage[slot, rows, pl.ds(src * heads + p * half, half), :] = x
+                if p == halves - 1:
+                    put(a, slot, r).start()
+                return 0
+
+            lax.fori_loop(0, strips, one, 0)
         return 0
 
     lax.fori_loop(0, 3, gather, 0)

time: 85.3 us -> 83.5 us (0.979)
  Pallas kernels: 84.5 us -> 82.7 us
    pallas_call x1, Pallas kernels: 81.1 us -> 79.3 us  [exchange(): pl.pallas_call(functools.partial(main_kernel, nseq, nhead, nsub), out_sha...]
where the time goes in v3:
time: 83.5 us; the launch traced here: 83.3 us
  Pallas kernels  82.7 us (99%)
    pallas_call x1, Pallas kernels, exchange(): pl.pallas_call(functools.partial(main_kernel, nseq, nhead, nsub), out_sha...  79.3 us
    pallas_call x1, Pallas kernels, finish(): pl.pallas_call(functools.partial(finish_kernel, pieces), out_shape=(jax.S...  3.42 us

profile of v3, /device:TPU:17, one launch (start us, length us, event | category | flops | bytes accessed | tf_op | source)
XLA Modules:
  0.0 83.3 jit_solution(15015799836381859285)
XLA Ops:
  0.6 79.3 %shard_map.75 = (bf16[512,16,128]{2,1,0:T(8,128)(2,1)S(1)}, bf16[3,128,64,128]{3,2,1,0:T(8,128)(2,1)S(1)}) custom-call(bf16[512,16,128]{2,1,0:T(8,128)(2,1)} %k_hbm.1, bf16[512,16,128]{2,1,0:T(8,128)(2,1)} %v_hbm.1, bf16[512,16,128]{2,1,0:T(8,128)(2,1)} %d_hbm.1, bf16[512,16,128]{2,1,0:T(8,128)(2,1)} %q_hbm.1), custom_call_target="tpu_custom_call" | custom-call | tf_op jit(solution)/shard_map/pallas_call | solution.py:376
  79.9 3.4 %shard_map.76 = (bf16[512,16,128]{2,1,0:T(8,128)(2,1)}, bf16[128,64,128]{2,1,0:T(8,128)(2,1)}, bf16[128,64,128]{2,1,0:T(8,128)(2,1)}, bf16[128,64,128]{2,1,0:T(8,128)(2,1)}) custom-call(bf16[512,16,128]{2,1,0:T(8,128)(2,1)S(1)} %get-tuple-element.6.att, bf16[3,128,64,128]{3,2,1,0:T(8,128)(2,1)S(1)} %get-tuple-element.7.grads), custom_call_target="tpu_custom_call" | custom-call | tf_op jit(solution)/shard_map/pallas_call | solution.py:430

commit v4 on v3

--- a/solution.py
+++ b/solution.py
@@ -8,7 +8,8 @@
 from jax.sharding import PartitionSpec as P
 
 MESH = pl.DeviceIdType.MESH
-CHUNK = 128
+CHUNK = 256
+LOAD = 128
 GROUP = 2
 F32 = jnp.float32
 BF16 = jnp.bfloat16
@@ -58,12 +59,12 @@
     sources = (k_hbm, v_hbm, d_hbm, q_hbm)
 
     def load(i, c):
-        rows = pl.ds(pl.multiple_of(c * CHUNK, CHUNK), CHUNK)
+        rows = pl.ds(pl.multiple_of(c * LOAD, LOAD), LOAD)
         return pltpu.make_async_copy(sources[i].at[rows], raw.at[i, rows], in_sem.at[i, c])
 
     def load_all(order):
         for i in order:
-            for c in range(chunks):
+            for c in range(tok // LOAD):
                 load(i, c).start()
 
     @pl.when(lower)
@@ -100,15 +101,15 @@
         def one(c, _):
             if wait:
                 load(i, c).wait()
-            for b in range(CHUNK // block):
-                rows = pl.ds(pl.multiple_of(c * CHUNK + b * block, block), block)
+            for b in range(LOAD // block):
+                rows = pl.ds(pl.multiple_of(c * LOAD + b * block, block), block)
                 x = jnp.swapaxes(raw[i, rows, some(p), :], 0, 1)
                 if i == 3:
                     x = (x.astype(F32) * fac[rows][None]).astype(BF16)
                 out[some(p), rows, :] = x
             return 0
 
-        lax.fori_loop(0, chunks, one, 0)
+        lax.fori_loop(0, tok // LOAD, one, 0)
 
     def part(c):
         return pl.ds(c * CHUNK, CHUNK)
@@ -394,7 +395,7 @@
             pltpu.VMEM((3, n, heads, tok_out, dim), BF16),
             pltpu.VMEM((2, tok_out, n * heads, dim), BF16),
             turned,
-            pltpu.SemaphoreType.DMA((4, chunks)),
+            pltpu.SemaphoreType.DMA((4, tok // LOAD)),
             pltpu.SemaphoreType.DMA((2, groups)),
             pltpu.SemaphoreType.DMA((2, groups)),
             pltpu.SemaphoreType.DMA((3, groups, n)),

time: 83.5 us -> 83.7 us (level)
  no operation moved by 1% of the time
where the time goes in v4:
time: 83.7 us; the launch traced here: 83.6 us
  Pallas kernels  83 us (99%)
    pallas_call x1, Pallas kernels, exchange(): pl.pallas_call(functools.partial(main_kernel, nseq, nhead, nsub), out_sha...  79.5 us
    pallas_call x1, Pallas kernels, finish(): pl.pallas_call(functools.partial(finish_kernel, pieces), out_shape=(jax.S...  3.42 us

profile of v4, /device:TPU:17, one launch (start us, length us, event | category | flops | bytes accessed | tf_op | source)
XLA Modules:
  0.0 83.6 jit_solution(18328617191802282053)
XLA Ops:
  0.6 79.5 %shard_map.75 = (bf16[512,16,128]{2,1,0:T(8,128)(2,1)S(1)}, bf16[3,128,64,128]{3,2,1,0:T(8,128)(2,1)S(1)}) custom-call(bf16[512,16,128]{2,1,0:T(8,128)(2,1)} %k_hbm.1, bf16[512,16,128]{2,1,0:T(8,128)(2,1)} %v_hbm.1, bf16[512,16,128]{2,1,0:T(8,128)(2,1)} %d_hbm.1, bf16[512,16,128]{2,1,0:T(8,128)(2,1)} %q_hbm.1), custom_call_target="tpu_custom_call" | custom-call | tf_op jit(solution)/shard_map/pallas_call | solution.py:377
  80.2 3.4 %shard_map.76 = (bf16[512,16,128]{2,1,0:T(8,128)(2,1)}, bf16[128,64,128]{2,1,0:T(8,128)(2,1)}, bf16[128,64,128]{2,1,0:T(8,128)(2,1)}, bf16[128,64,128]{2,1,0:T(8,128)(2,1)}) custom-call(bf16[512,16,128]{2,1,0:T(8,128)(2,1)S(1)} %get-tuple-element.6.att, bf16[3,128,64,128]{3,2,1,0:T(8,128)(2,1)S(1)} %get-tuple-element.7.grads), custom_call_target="tpu_custom_call" | custom-call | tf_op jit(solution)/shard_map/pallas_call | solution.py:431

commit v5 on v3

--- a/solution.py
+++ b/solution.py
@@ -68,11 +68,11 @@
 
     @pl.when(lower)
     def _():
-        load_all((0, 1, 2, 3))
+        load_all((0, 1))
 
     @pl.when(upper)
     def _():
-        load_all((2, 3, 1, 0))
+        load_all((2, 3))
 
     row = lax.broadcasted_iota(jnp.int32, (tok, dim), 0)
     fac[...] = lax.rsqrt(F32(dim) * (seq * tok + row + 1).astype(F32))
@@ -197,10 +197,6 @@
     def walk(way, a, compute, begin, end, first):
         def one(g, _):
             if first:
-                @pl.when(g + 1 < end)
-                def _():
-                    total(way, g + 1)
-
                 pass_on(way, g)
             edge, loc = (pre_in, kv_loc) if way == 0 else (suf_in, ad_loc)
             for i in range(size):
@@ -210,6 +206,11 @@
                     state = (outer + loc[h, c]).astype(BF16)
                     grads[a, h, part(c)] = compute(h, c, state).astype(BF16)
             send(a, g)
+            if first:
+                @pl.when(g + 1 < end)
+                def _():
+                    total(way, g + 1)
+
             return 0
 
         lax.fori_loop(begin, end, one, 0)
@@ -237,12 +238,16 @@
     @pl.when(lower)
     def _():
         turn(0, 0, True)
+        load_all((2,))
         turn(1, 0, True)
+        load_all((3,))
 
     @pl.when(upper)
     def _():
         turn(2, 0, True)
+        load_all((1,))
         turn(3, 0, True)
+        load_all((0,))
 
     pl.semaphore_wait(
         barrier, n - 1 + (seq > 0).astype(jnp.int32) + (seq < last).astype(jnp.int32)

time: 83.5 us -> 83.6 us (level)
  no operation moved by 1% of the time
where the time goes in v5:
time: 83.6 us; the launch traced here: 83.5 us
  Pallas kernels  82.8 us (99%)
    pallas_call x1, Pallas kernels, exchange(): pl.pallas_call(functools.partial(main_kernel, nseq, nhead, nsub), out_sha...  79.4 us
    pallas_call x1, Pallas kernels, finish(): pl.pallas_call(functools.partial(finish_kernel, pieces), out_shape=(jax.S...  3.42 us

profile of v5, /device:TPU:17, one launch (start us, length us, event | category | flops | bytes accessed | tf_op | source)
XLA Modules:
  0.0 83.5 jit_solution(11973399179302627206)
XLA Ops:
  0.6 79.4 %shard_map.75 = (bf16[512,16,128]{2,1,0:T(8,128)(2,1)S(1)}, bf16[3,128,64,128]{3,2,1,0:T(8,128)(2,1)S(1)}) custom-call(bf16[512,16,128]{2,1,0:T(8,128)(2,1)} %k_hbm.1, bf16[512,16,128]{2,1,0:T(8,128)(2,1)} %v_hbm.1, bf16[512,16,128]{2,1,0:T(8,128)(2,1)} %d_hbm.1, bf16[512,16,128]{2,1,0:T(8,128)(2,1)} %q_hbm.1), custom_call_target="tpu_custom_call" | custom-call | tf_op jit(solution)/shard_map/pallas_call | solution.py:381
  80.1 3.4 %shard_map.76 = (bf16[512,16,128]{2,1,0:T(8,128)(2,1)}, bf16[128,64,128]{2,1,0:T(8,128)(2,1)}, bf16[128,64,128]{2,1,0:T(8,128)(2,1)}, bf16[128,64,128]{2,1,0:T(8,128)(2,1)}) custom-call(bf16[512,16,128]{2,1,0:T(8,128)(2,1)S(1)} %get-tuple-element.6.att, bf16[3,128,64,128]{3,2,1,0:T(8,128)(2,1)S(1)} %get-tuple-element.7.grads), custom_call_target="tpu_custom_call" | custom-call | tf_op jit(solution)/shard_map/pallas_call | solution.py:435

commit v6 on v3

--- a/solution.py
+++ b/solution.py
@@ -21,7 +21,7 @@
 def main_kernel(
     nseq, nhead, nsub,
     k_hbm, v_hbm, d_hbm, q_hbm,
-    att_out, grad_out,
+    att_out, grad_out, final,
     raw, kt, vt, dt, qt, fac, kv_loc, kv_tot, ad_loc, ad_tot,
     pre_in, pre_out, suf_in, suf_out, grads, held, stage, att,
     in_sem, z_send, z_recv, x_send, x_recv, own_sem, att_sem, out_sem,
@@ -165,12 +165,15 @@
         rows = pl.ds(pl.multiple_of(other * tok_out, tok_out), tok_out)
         return grads.at[a, group(g), rows]
 
+    def landing(a, src, g):
+        return held.at[a, src, group(g)] if a < 2 else final.at[src, group(g)]
+
     def cross(a, g, off, arriving=False):
         other, ids = mate(off)
         src = other if arriving else me
         return pltpu.make_async_remote_copy(
             src_ref=mine(a, g, other),
-            dst_ref=held.at[a, src, group(g)],
+            dst_ref=landing(a, src, g),
             send_sem=x_send.at[a, g, other],
             recv_sem=x_recv.at[a, g, src],
             device_id=ids,
@@ -178,7 +181,7 @@
         )
 
     def own(a, g):
-        return pltpu.make_async_copy(mine(a, g, me), held.at[a, me, group(g)], own_sem.at[a, g])
+        return pltpu.make_async_copy(mine(a, g, me), landing(a, me, g), own_sem.at[a, g])
 
     def send(a, g):
         for off in offsets:
@@ -270,10 +273,10 @@
 
     @pl.when(upper)
     def _():
-        open_walk(1, 1, key_part, (2, 3), 1)
+        open_walk(1, 0, key_part, (2, 3), 1)
         turn_whole(0)
-        walk_all(1, 2, value_part, False)
-        walk_all(0, 0, query_part, True)
+        walk_all(1, 1, value_part, False)
+        walk_all(0, 2, query_part, True)
 
     def attend(g, _):
         for i in range(size):
@@ -301,47 +304,36 @@
     strip = min(16, tok_out)
     strips = tok_out // strip
 
-    def put(a, slot, r):
+    def put(slot, r):
         rows = pl.ds(pl.multiple_of(r * strip, strip), strip)
         return pltpu.make_async_copy(
-            stage.at[slot, rows], grad_out.at[a, rows], out_sem.at[slot, r]
-        )
-
-    def gather(i, _):
-        a = lax.rem(i + upper.astype(jnp.int32), 3)
-        slot = lax.rem(i, 2)
-
-        @pl.when(i >= 2)
-        def _():
-            for r in range(strips):
-                put(a, slot, r).wait()
-
+            stage.at[slot, rows], grad_out.at[slot, rows], out_sem.at[slot, r]
+        )
+
+    for a in range(3):
         def arrive(g, _):
             own(a, g).wait()
             for off in offsets:
                 cross(a, g, off, True).wait_recv()
             return 0
 
+        def one(p, r, _):
+            rows = pl.ds(pl.multiple_of(r * strip, strip), strip)
+            if halves == 1:
+                x = held[a, :, :, rows, :].reshape(n * heads, strip, dim)
+                stage[a, rows] = jnp.swapaxes(x, 0, 1)
+            else:
+                for src in range(n):
+                    x = jnp.swapaxes(held[a, src, some(p), rows, :], 0, 1)
+                    stage[a, rows, pl.ds(src * heads + p * half, half), :] = x
+            if p == halves - 1:
+                put(a, r).start()
+            return 0
+
         for p in range(halves):
             lax.fori_loop(p * half_groups, (p + 1) * half_groups, arrive, 0)
-
-            def one(r, _):
-                rows = pl.ds(pl.multiple_of(r * strip, strip), strip)
-                if halves == 1:
-                    x = held[a, :, :, rows, :].reshape(n * heads, strip, dim)
-                    stage[slot, rows] = jnp.swapaxes(x, 0, 1)
-                else:
-                    for src in range(n):
-                        x = jnp.swapaxes(held[a, src, some(p), rows, :], 0, 1)
-                        stage[slot, rows, pl.ds(src * heads + p * half, half), :] = x
-                if p == halves - 1:
-                    put(a, slot, r).start()
-                return 0
-
-            lax.fori_loop(0, strips, one, 0)
-        return 0
-
-    lax.fori_loop(0, 3, gather, 0)
+            if a < 2:
+                lax.fori_loop(0, strips, functools.partial(one, p), 0)
 
     def drain(g, _):
         @pl.when(seq < last)
@@ -360,7 +352,7 @@
     lax.fori_loop(0, groups, drain, 0)
     for slot in range(2):
         for r in range(strips):
-            put(0, slot, r).wait()
+            put(slot, r).wait()
     att_copy.wait()
 
 
@@ -377,10 +369,11 @@
         functools.partial(main_kernel, nseq, nhead, nsub),
         out_shape=(
             pltpu.VMEM((tok, heads, dim), BF16),
-            pltpu.VMEM((3, tok_out, n * heads, dim), BF16),
+            pltpu.VMEM((2, tok_out, n * heads, dim), BF16),
+            pltpu.VMEM((n, heads, tok_out, dim), BF16),
         ),
         in_specs=[any_spec] * 4,
-        out_specs=(any_spec,) * 2,
+        out_specs=(any_spec,) * 3,
         scratch_shapes=[
             pltpu.VMEM((4, tok, heads, dim), BF16),
             turned, turned, turned, turned,
@@ -391,7 +384,7 @@
             pltpu.VMEM((heads, dim, dim), F32),
             low, low, low, low,
             pltpu.VMEM((3, heads, tok, dim), BF16),
-            pltpu.VMEM((3, n, heads, tok_out, dim), BF16),
+            pltpu.VMEM((2, n, heads, tok_out, dim), BF16),
             pltpu.VMEM((2, tok_out, n * heads, dim), BF16),
             turned,
             pltpu.SemaphoreType.DMA((4, chunks)),
@@ -404,38 +397,87 @@
             pltpu.SemaphoreType.DMA((2, tok_out // min(16, tok_out))),
         ],
         compiler_params=pltpu.CompilerParams(
-            collective_id=0, has_side_effects=True, vmem_limit_bytes=50 * 2**20
+            collective_id=0, has_side_effects=True, vmem_limit_bytes=48 * 2**20
         ),
     )(key_rows, value_rows, out_adjoint, queries)
 
 
-def finish_kernel(pieces, att, grads, att_out, a_out, b_out, c_out, sem):
-    outs = (att_out, a_out, b_out, c_out)
-    copies = []
-    for i, dst in enumerate(outs):
-        src = att if i == 0 else grads.at[i - 1]
+def finish_kernel(
+    nseq, pieces, att, grads, late, att_out, qg_out, kg_out, vg_out, buf, stage, sem, in_sem, out_sem
+):
+    lower = lax.axis_index("seq") < (nseq + 1) // 2
+    upper = jnp.logical_not(lower)
+    n, heads, tok_out, dim = late.shape
+    strip = tok_out // pieces
+
+    def strip_rows(p):
+        return pl.ds(p * strip, strip)
+
+    def fetch(p):
+        return pltpu.make_async_copy(
+            late.at[:, :, strip_rows(p)], buf.at[:, :, strip_rows(p)], in_sem.at[p]
+        )
+
+    def copies(i, src, dst):
         step = dst.shape[0] // pieces
+        rows = [pl.ds(p * step, step) for p in range(pieces)]
+        return [
+            pltpu.make_async_copy(src.at[r], dst.at[r], sem.at[i, p]) for p, r in enumerate(rows)
+        ]
+
+    def put(dst, p):
+        return pltpu.make_async_copy(
+            stage.at[strip_rows(p)], dst.at[strip_rows(p)], out_sem.at[p]
+        )
+
+    def turn(p):
+        x = buf[:, :, strip_rows(p), :].reshape(n * heads, strip, dim)
+        stage[strip_rows(p)] = jnp.swapaxes(x, 0, 1)
+
+    def run(first, second, final):
         for p in range(pieces):
-            rows = pl.ds(p * step, step)
-            copies.append(pltpu.make_async_copy(src.at[rows], dst.at[rows], sem.at[i, p]))
-    for copy in copies:
-        copy.start()
-    for copy in copies:
-        copy.wait()
-
-
-def finish(att, grads):
-    pieces = 4
+            fetch(p).start()
+        rest = copies(0, grads.at[0], first) + copies(1, grads.at[1], second)
+        rest += copies(2, att, att_out)
+        for copy in rest:
+            copy.start()
+        for p in range(pieces):
+            fetch(p).wait()
+            turn(p)
+            put(final, p).start()
+        for copy in rest:
+            copy.wait()
+        for p in range(pieces):
+            put(final, p).wait()
+
+    @pl.when(lower)
+    def _():
+        run(qg_out, kg_out, vg_out)
+
+    @pl.when(upper)
+    def _():
+        run(kg_out, vg_out, qg_out)
+
+
+def finish(nseq, att, grads, late):
+    tok_out = late.shape[2]
+    pieces = max(1, min(4, tok_out // 16))
     any_spec = pl.BlockSpec(memory_space=pl.ANY)
     return pl.pallas_call(
-        functools.partial(finish_kernel, pieces),
+        functools.partial(finish_kernel, nseq, pieces),
         out_shape=(jax.ShapeDtypeStruct(att.shape, BF16),)
         + (jax.ShapeDtypeStruct(grads.shape[1:], BF16),) * 3,
-        in_specs=[any_spec] * 2,
+        in_specs=[any_spec] * 3,
         out_specs=(any_spec,) * 4,
-        scratch_shapes=[pltpu.SemaphoreType.DMA((4, pieces))],
-        compiler_params=pltpu.CompilerParams(vmem_limit_bytes=2**20),
-    )(att, grads)
+        scratch_shapes=[
+            pltpu.VMEM(late.shape, BF16),
+            pltpu.VMEM(grads.shape[1:], BF16),
+            pltpu.SemaphoreType.DMA((3, pieces)),
+            pltpu.SemaphoreType.DMA((pieces,)),
+            pltpu.SemaphoreType.DMA((pieces,)),
+        ],
+        compiler_params=pltpu.CompilerParams(vmem_limit_bytes=12 * 2**20),
+    )(att, grads, late)
 
 
 def solution(mesh):
@@ -444,10 +486,11 @@
 
     def per_device(queries, key_rows, value_rows, out_adjoint):
         return finish(
+            mesh.shape["seq"],
             *exchange(
                 mesh.shape["seq"], mesh.shape["head"], mesh.shape["sub"],
                 queries, key_rows, value_rows, out_adjoint,
-            )
+            ),
         )
 
     return jax.shard_map(

time: 83.5 us -> 83.4 us (level)
  no operation moved by 1% of the time
where the time goes in v6:
time: 83.4 us; the launch traced here: 83.3 us
  Pallas kernels  82.6 us (99%)
    pallas_call x1, Pallas kernels, exchange(): pl.pallas_call(functools.partial(main_kernel, nseq, nhead, nsub), out_sha...  78.7 us
    pallas_call x1, Pallas kernels, finish(): pl.pallas_call(functools.partial(finish_kernel, nseq, pieces), out_shape=...  3.97 us

profile of v6, /device:TPU:17, one launch (start us, length us, event | category | flops | bytes accessed | tf_op | source)
XLA Modules:
  0.0 83.3 jit_solution(14280281835335098645)
XLA Ops:
  0.6 78.7 %shard_map.75 = (bf16[512,16,128]{2,1,0:T(8,128)(2,1)S(1)}, bf16[2,128,64,128]{3,2,1,0:T(8,128)(2,1)S(1)}, bf16[4,16,128,128]{3,2,1,0:T(8,128)(2,1)S(1)}) custom-call(bf16[512,16,128]{2,1,0:T(8,128)(2,1)} %k_hbm.1, bf16[512,16,128]{2,1,0:T(8,128)(2,1)} %v_hbm.1, bf16[512,16,128]{2,1,0:T(8,128)(2,1)} %d_hbm.1, bf16[512,16,128]{2,1,0:T(8,128)(2,1)} %q_hbm.1), custom_call_target="tpu_custom_call" | custom-call | tf_op jit(solution)/shard_map/pallas_call | solution.py:368
  79.3 4.0 %shard_map.76 = (bf16[512,16,128]{2,1,0:T(8,128)(2,1)}, bf16[128,64,128]{2,1,0:T(8,128)(2,1)}, bf16[128,64,128]{2,1,0:T(8,128)(2,1)}, bf16[128,64,128]{2,1,0:T(8,128)(2,1)}) custom-call(bf16[512,16,128]{2,1,0:T(8,128)(2,1)S(1)} %get-tuple-element.7.att, bf16[2,128,64,128]{3,2,1,0:T(8,128)(2,1)S(1)} %get-tuple-element.8.grads, ...), custom_call_target="tpu_custom_call" | custom-call | tf_op jit(solution)/shard_map/pallas_call | solution.py:466
